TPU v7x, 32 devices: a whole 2x2x4 slice. The times are simulated.
32 devices in a mesh: groups: 2 (over y), dp: 4 (over z), mp: 2 (over x), sub: 2 (over core).
Axes of the slice: x: 2, y: 2, z: 4, core: 2. Of those that a mesh axis runs over, the one named last changes fastest.
Arguments:
- tokens_in: bfloat16 [128, 4096], P(('groups', 'dp'), ('mp', 'sub')), parts along dimension 0, may hold values from -6 to 6
- grad_out: bfloat16 [128, 4096], P(('groups', 'dp'), ('mp', 'sub')), parts along dimension 0, may hold values from -12 to 12
- sample_grad: bfloat16 [128, 4096], P(('groups', 'dp'), ('mp', 'sub')), parts along dimension 0, may hold values from -4.5 to 4.5
- gate_tiles: bfloat16 [256, 16, 128, 128], P(('groups', 'dp'), ('mp', 'sub')), parts along dimension 0, may hold values from -0.125 to 0.125
- up_tiles: bfloat16 [256, 16, 128, 128], P(('groups', 'dp'), ('mp', 'sub')), parts along dimension 0, may hold values from -0.125 to 0.125
- down_tiles: bfloat16 [256, 16, 128, 128], P(('groups', 'dp'), ('mp', 'sub')), parts along dimension 0, may hold values from -0.0625 to 0.0625
- block_index: int32 [6, 128, 16], P('groups', 'dp', ('mp', 'sub')), parts along dimension 0, may hold values from 0 to 31, as said below
- owner_map: int32 [4, 128, 16], P('groups', 'dp', ('mp', 'sub')), parts along dimension 0, may hold values from 0 to 3, as said below
- slot_map: int32 [4, 128, 16], P('groups', 'dp', ('mp', 'sub')), parts along dimension 0, may hold values from 0 to 383, as said below
- moment_state: bfloat16 [8, 4, 384, 128, 128], P(('groups', 'dp'), ('mp', 'sub')), parts along dimension 0, may hold values from -0.59765625 to 0.59765625
- curvature_state: bfloat16 [8, 4, 384, 128, 128], P(('groups', 'dp'), ('mp', 'sub')), parts along dimension 0, may hold values from 0.0099487305 to 1
Outputs:
- new_moment: bfloat16 [8, 4, 384, 128, 128], P(('groups', 'dp'), ('mp', 'sub')), parts along dimension 0
- new_curvature: bfloat16 [8, 4, 384, 128, 128], P(('groups', 'dp'), ('mp', 'sub')), parts along dimension 0
- update: bfloat16 [8, 4, 384, 128, 128], P(('groups', 'dp'), ('mp', 'sub')), parts along dimension 0
There are 2 independent parts, one for each index of `groups`. A program takes and returns all parts, laid end to end along the dimension named above; each array names one. Nothing has to cross between parts.
Inputs may be any that keep to these rules, and one draw needn't show every extreme that they name: `block_index`: for each matrix m and hidden block c, the entries k with k // 4 = g are 4 distinct width blocks in [g * 8, (g + 1) * 8). `owner_map`: the blocks of one device are those with c // 32 equal to its dp index and k // 4 equal to its band. Of one device's gate and up blocks together, at most 128 have the same owner, and in every draw some device has exactly 128 with one owner. `slot_map`: within one band, blocks with the same owner have distinct slots; an owner receives at most 384 blocks of a band, and in every band some owner receives exactly 384.
All inputs are finite; a program needn't handle non-finite values.
Results may differ from a plain program's by a relative error of at most 0.035.
Values may be sent and summed in bfloat16 or wider, within the bound.
A program may use at most 320 MiB of HBM per device.

v0:
```python
import jax
import jax.numpy as jnp
from jax import lax
from jax.sharding import PartitionSpec as P

momentum_decay = 0.9
curvature_decay = 0.95
curvature_scale = 0.5


def pick_blocks(matrix, row_list, block_size):
    shaped = matrix.reshape(matrix.shape[0], matrix.shape[1] // block_size, block_size)
    return jnp.take(shaped, row_list, axis=1)


def backward_signals(summed):
    hidden_width = summed.shape[1] // 4
    gate_sum = summed[:, 0:hidden_width]
    up_sum = summed[:, hidden_width : 2 * hidden_width]
    hidden_grad = summed[:, 2 * hidden_width : 3 * hidden_width]
    sample_hidden = summed[:, 3 * hidden_width : 4 * hidden_width]
    sigmoid_gate = jax.nn.sigmoid(gate_sum)
    activation = gate_sum * sigmoid_gate
    gate_slope = up_sum * sigmoid_gate * (1.0 + gate_sum * (1.0 - sigmoid_gate))
    return jnp.concatenate(
        [
            hidden_grad * gate_slope,
            hidden_grad * activation,
            sample_hidden * gate_slope,
            sample_hidden * activation,
        ],
        axis=1,
    ).astype(jnp.bfloat16)


def on_device(
    tokens_in,
    grad_out,
    sample_grad,
    gate_tiles,
    up_tiles,
    down_tiles,
    block_index,
    owner_map,
    slot_map,
    moment_state,
    curvature_state,
):
    block_size = gate_tiles.shape[-1]
    column_count = gate_tiles.shape[0]
    band_blocks = tokens_in.shape[1] // block_size
    hidden_width = column_count * block_size
    all_tokens, all_grads, all_samples = (
        lax.all_gather(tokens_in, "dp", axis=0, tiled=True),
        lax.all_gather(grad_out, "dp", axis=0, tiled=True),
        lax.all_gather(sample_grad, "dp", axis=0, tiled=True),
    )
    token_count = all_tokens.shape[0]
    local_rows = block_index - lax.axis_index(("mp", "sub")) * band_blocks
    token_rows = all_tokens
    gate_part = jnp.einsum(
        "tckd,ckde->tce",
        pick_blocks(token_rows, local_rows[0], block_size),
        gate_tiles,
        preferred_element_type=jnp.float32,
    )
    up_part = jnp.einsum(
        "tckd,ckde->tce",
        pick_blocks(token_rows, local_rows[1], block_size),
        up_tiles,
        preferred_element_type=jnp.float32,
    )
    down_part = jnp.einsum(
        "tckd,cked->tce",
        pick_blocks(all_grads, local_rows[2], block_size),
        down_tiles,
        preferred_element_type=jnp.float32,
    )
    sample_part = jnp.einsum(
        "tckd,cked->tce",
        pick_blocks(all_samples, local_rows[2], block_size),
        down_tiles,
        preferred_element_type=jnp.float32,
    )
    summed = lax.psum(
        jnp.concatenate([gate_part, up_part, down_part, sample_part], axis=1)
        .reshape(token_count, 4 * hidden_width)
        .astype(jnp.bfloat16),
        ("mp", "sub"),
    ).astype(jnp.float32)
    shard_rows = backward_signals(summed)
    row_count = shard_rows.shape[0]
    token_rows = all_tokens
    gate_rows = pick_blocks(token_rows, local_rows[0], block_size)
    up_rows = pick_blocks(token_rows, local_rows[1], block_size)
    signals = shard_rows.reshape(row_count, 4, column_count, block_size)
    grad_gate = jnp.einsum(
        "tckd,tce->ckde", gate_rows, signals[:, 0], preferred_element_type=jnp.float32
    )
    grad_up = jnp.einsum(
        "tckd,tce->ckde", up_rows, signals[:, 1], preferred_element_type=jnp.float32
    )
    hat_gate = jnp.einsum(
        "tckd,tce->ckde", gate_rows, signals[:, 2], preferred_element_type=jnp.float32
    )
    hat_up = jnp.einsum(
        "tckd,tce->ckde", up_rows, signals[:, 3], preferred_element_type=jnp.float32
    )
    totals = jnp.stack([jnp.stack([grad_gate, grad_up]), jnp.stack([hat_gate, hat_up])])
    tile_list = jnp.transpose(totals.astype(jnp.bfloat16), (1, 2, 3, 0, 4, 5)).reshape(
        -1, 2, block_size, block_size
    )
    tile_total = tile_list.shape[0]
    owner_count = lax.axis_size("dp")
    own_cap = moment_state.shape[2]
    send_cap = max(2, 2 * (tile_total // owner_count))
    owners = owner_map.reshape(-1)
    slot_list = slot_map.reshape(-1)
    same_owner = owners[:, None] == owners[None, :]
    earlier = jnp.arange(tile_total)[None, :] < jnp.arange(tile_total)[:, None]
    send_rank = jnp.sum((same_owner & earlier).astype(jnp.int32), axis=1)
    position = owners * send_cap + send_rank
    payload = (
        jnp.zeros((owner_count * send_cap, 2, block_size, block_size), jnp.bfloat16)
        .at[position]
        .set(tile_list)
    )
    slot_ids = jnp.full((owner_count * send_cap,), own_cap, jnp.int32).at[position].set(slot_list)
    received, received_ids = (
        lax.all_to_all(
            payload.reshape(owner_count, send_cap, 2, block_size, block_size),
            "dp",
            split_axis=0,
            concat_axis=0,
            tiled=True,
        ),
        lax.all_to_all(
            slot_ids.reshape(owner_count, send_cap), "dp", split_axis=0, concat_axis=0, tiled=True
        ),
    )
    placed = jnp.zeros((own_cap + 1, 2, block_size, block_size), jnp.bfloat16)
    placed = placed.at[received_ids.reshape(-1)].set(
        received.reshape(-1, 2, block_size, block_size)
    )[:own_cap]
    grad_state = placed[:, 0].astype(jnp.float32)
    hat_state = placed[:, 1].astype(jnp.float32)
    state_shape = moment_state.shape
    moment = (
        momentum_decay * moment_state.reshape(own_cap, block_size, block_size).astype(jnp.float32)
        + (1.0 - momentum_decay) * grad_state
    )
    curvature = (
        curvature_decay
        * curvature_state.reshape(own_cap, block_size, block_size).astype(jnp.float32)
        + (1.0 - curvature_decay) * hat_state * hat_state
    )
    update = jnp.clip(moment / (curvature_scale * curvature), -1.0, 1.0)
    return (
        moment.astype(jnp.bfloat16).reshape(state_shape),
        curvature.astype(jnp.bfloat16).reshape(state_shape),
        update.astype(jnp.bfloat16).reshape(state_shape),
    )


def solution(mesh):
    in_specs = (
        P(("groups", "dp"), ("mp", "sub")),
        P(("groups", "dp"), ("mp", "sub")),
        P(("groups", "dp"), ("mp", "sub")),
        P(("groups", "dp"), ("mp", "sub"), None, None),
        P(("groups", "dp"), ("mp", "sub"), None, None),
        P(("groups", "dp"), ("mp", "sub"), None, None),
        P("groups", "dp", ("mp", "sub")),
        P("groups", "dp", ("mp", "sub")),
        P("groups", "dp", ("mp", "sub")),
        P(("groups", "dp"), ("mp", "sub"), None, None, None),
        P(("groups", "dp"), ("mp", "sub"), None, None, None),
    )
    out_specs = (
        P(("groups", "dp"), ("mp", "sub"), None, None, None),
        P(("groups", "dp"), ("mp", "sub"), None, None, None),
        P(("groups", "dp"), ("mp", "sub"), None, None, None),
    )
    return jax.shard_map(
        on_device, mesh=mesh, in_specs=in_specs, out_specs=out_specs, check_vma=False
    )
```

profile of v0, /device:TPU:0, one launch (start us, length us, event | category | flops | bytes accessed | tf_op | source)
XLA Modules:
  0.0 1079.7 jit_solution(108160368596566791)
XLA Ops:
  7.2 0.0 all-reduce.2.cloned.1.call-start
  7.2 0.7 broadcast_subtract_fusion
  7.9 0.1 copy.70
  8.0 0.1 reshape.231
  8.1 15.3 %all_gather.9 = bf16[64,1024]{1,0:T(8,128)(2,1)S(1)} all-gather(bf16[16,1024]{1,0:T(8,128)(2,1)} %param.13), channel_id=1, replica_groups=mesh['groups'=2,'dp'=4,'mp'=2,'sub'=2] {'dp'}, dimensions={0}, use_global_device_ids=true | all-gather | bytes 163840 | tf_op jit(solution)/shard_map/all_gather | solution.py:54
  23.4 0.1 copy.69
  23.5 0.1 copy.73
  23.6 0.1 reshape.235
  23.8 0.0 copy-start.5
  23.8 1.0 gather_fusion
  24.7 2.1 gather_fusion.1
  26.9 0.1 copy.72
  27.0 0.1 copy.76
  27.1 0.1 reshape.239
  27.2 13.6 %all_gather.10 = bf16[64,1024]{1,0:T(8,128)(2,1)S(1)} all-gather(bf16[16,1024]{1,0:T(8,128)(2,1)S(1)} %copy-done.4), channel_id=1, replica_groups=mesh['groups'=2,'dp'=4,'mp'=2,'sub'=2] {'dp'}, dimensions={0}, use_global_device_ids=true | all-gather | bytes 163840 | tf_op jit(solution)/shard_map/all_gather | solution.py:55
  40.8 0.1 copy.75
  40.9 13.3 %all_gather.11 = bf16[64,1024]{1,0:T(8,128)(2,1)S(1)} all-gather(bf16[16,1024]{1,0:T(8,128)(2,1)S(1)} %copy-done.5), channel_id=1, replica_groups=mesh['groups'=2,'dp'=4,'mp'=2,'sub'=2] {'dp'}, dimensions={0}, use_global_device_ids=true | all-gather | bytes 163840 | tf_op jit(solution)/shard_map/all_gather | solution.py:56
  54.3 2.1 gather_fusion.2
  56.4 2.1 gather_fusion.3
  58.6 4.6 fusion.49
  63.1 0.0 copy-start.9
  63.2 0.1 copy-done.8
  63.2 1.6 fusion.52
  64.8 0.0 copy-start
  64.9 0.5 copy-done.9
  65.4 0.9 fusion.43
  66.3 0.3 copy-done
  66.6 1.2 copy-done.10
  67.8 0.9 fusion.46
  68.7 0.0 copy-start.6
  68.7 0.0 copy-start.7
  68.7 1.6 copy_bitcast_fusion
  70.3 0.0 all-reduce.2.cloned.1.call-update
  70.3 0.1 copy.67
  70.4 0.1 copy.66
  70.5 0.1 mul.115
  70.6 0.1 eq.15
  70.8 0.1 copy.68
  70.9 0.1 reshape.203
  71.0 0.2 convert_reduce_fusion
  71.2 2.0 scatter_custom_fusion
  73.1 4.9 all-to-all-start
  78.0 45.1 %all-reduce.2.cloned.1.call-done = bf16[64,16384]{1,0:T(8,128)(2,1)} async-done(((bf16[64,16384]{1,0:T(8,128)(2,1)}), bf16[64,16384]{1,0:T(8,128)(2,1)}) %all-reduce.2.cloned.1.call-update) | async-done | bytes 2097168 | tf_op jit(solution)/shard_map/psum | solution.py:85
  123.2 1.9 convert_element_type.64
  125.0 0.7 fusion.65
  125.8 0.1 copy.112
  125.9 0.7 copy-done.1
  126.6 1.6 convert_bitcast_fusion
  128.3 0.1 copy.111
  128.4 3.6 convert_bitcast_fusion.1
  132.0 0.1 copy.110
  132.1 1.6 convert_bitcast_fusion.2
  133.7 0.1 copy.109
  133.8 3.6 convert_bitcast_fusion.3
  137.4 3.7 maximum_bitcast_fusion
  141.2 1.7 pad_maximum_fusion
  142.9 6.5 copy.86
  149.4 11.3 %broadcast_in_dim.25 = bf16[512,2,128,128]{3,2,1,0:T(8,128)(2,1)} broadcast(bf16[]{:T(256)} %constant.25.clone.1), dimensions={} | broadcast | bytes 33554432 | tf_op jit(solution)/shard_map/broadcast_in_dim | solution.py:124
  160.6 45.3 %scatter_fusion = bf16[512,2,128,128]{3,2,1,0:T(8,128)(2,1)} fusion(bf16[512,2,128,128]{3,2,1,0:T(8,128)(2,1)} %broadcast_in_dim.25, s32[256]{0:T(256)S(1)} %bitcast.204, bf16[256,2,128,128]{3,2,1,0:T(8,128)(2,1)} %copy.86), kind=kCustom, calls=%fused_computation.5 | custom fusion | bytes 50332672 | tf_op jit(solution)/shard_map/scatter | solution.py:126
  205.9 9.9 all-to-all-start.1
  215.9 722.4 %all-to-all-done.1 = bf16[4,128,2,128,128]{4,3,2,1,0:T(8,128)(2,1)} async-done(((bf16[4,128,2,128,128]{4,3,2,1,0:T(8,128)(2,1)}), bf16[4,128,2,128,128]{4,3,2,1,0:T(8,128)(2,1)}, u32[]{:S(2)}, u32[]{:S(2)}) %all-to-all-start.1) | async-done | bytes 33554464 | tf_op jit(solution)/shard_map/all_to_all | solution.py:130
  938.3 9.2 broadcast_in_dim.23
  947.4 92.4 %scatter_fusion.1 = bf16[385,2,128,128]{3,2,1,0:T(8,128)(2,1)} fusion(bf16[385,2,128,128]{3,2,1,0:T(8,128)(2,1)} %broadcast_in_dim.23, s32[512]{0:T(512)S(1)} %bitcast.202, bf16[512,2,128,128]{3,2,1,0:T(8,128)(2,1)} %bitcast.41), kind=kCustom, calls=%fused_computation.6 | custom fusion | bytes 100665344 | tf_op jit(solution)/shard_map/scatter | solution.py:142
  1039.8 33.0 %clamp_convert_fusion = (bf16[1,1,384,128,128]{4,3,2,1,0:T(8,128)(2,1)}, bf16[1,1,384,128,128]{4,3,2,1,0:T(8,128)(2,1)}, bf16[1,1,384,128,128]{4,3,2,1,0:T(8,128)(2,1)}) fusion(bf16[1,1,384,128,128]{4,3,2,1,0:T(8,128)(2,1)} %param.22, bf16[1,1,384,128,128]{4,3,2,1,0:T(8,128)(2,1)} %param.23, bf16[385,2,128,128]{3,2,1,0:T(8,128)(2,1)} %scatter_fusion.1), kind=kLoop, calls=%fused_computation.10 | loop fusion | flops 106954752 | bytes 88080384 | tf_op jit(solution)/shard_map/convert_element_type | solution.py:161
  (24 shorter events, 0.2 us)
Async XLA Ops:
  7.2 116.0 %all-reduce.2.cloned.1.call-start = ((), (), s32[]{:S(2)}) async-start(), calls=%async_computation.2 | async-start | bytes 4194304 | tf_op jit(solution)/shard_map/psum | solution.py:85
  23.8 3.4 copy-start.4
  23.8 17.2 %copy-start.5 = (bf16[16,1024]{1,0:T(8,128)(2,1)S(1)}, bf16[16,1024]{1,0:T(8,128)(2,1)}, u32[]{:S(2)}) copy-start(bf16[16,1024]{1,0:T(8,128)(2,1)} %param.15) | copy-start | bytes 98308
  58.6 4.6 copy-start.3
  58.6 4.7 copy-start.8
  63.1 2.2 copy-start.9
  64.8 1.7 copy-start
  64.8 2.9 copy-start.10
  68.7 1.6 copy-start.6
  68.7 2.1 copy-start.7
  73.1 132.8 %all-to-all-start = ((s32[4,1,128]{2,1,0:T(1,128)}), s32[4,1,128]{2,1,0:T(1,128)S(1)}, u32[]{:S(2)}, u32[]{:S(2)}) async-start(s32[4,1,128]{2,1,0:T(1,128)} %bitcast.2), calls=%async_computation | async-start | bytes 4096 | tf_op jit(solution)/shard_map/all_to_all | solution.py:137
  125.0 1.6 copy-start.1
  133.7 3.7 copy-start.2
  205.9 732.3 %all-to-all-start.1 = ((bf16[4,128,2,128,128]{4,3,2,1,0:T(8,128)(2,1)}), bf16[4,128,2,128,128]{4,3,2,1,0:T(8,128)(2,1)}, u32[]{:S(2)}, u32[]{:S(2)}) async-start(bf16[4,128,2,128,128]{4,3,2,1,0:T(8,128)(2,1)} %bitcast.188), calls=%async_computation.1 | async-start | bytes 67108864 | tf_op jit(solution)/shard_map/all_to_all | solution.py:130
Sparse Core Ops, SparseCore 0:
  70.4 52.6 all-reduce.1
where the time goes:
time: 1080 us
  waiting for transfers between devices  768 us (71%)
  local copies, waits for them, and re-layouts  179 us (17%)
  other arithmetic  43.6 us (4%)
  blocking collectives  42.2 us (4%)
  matrix products  18.5 us (2%)
  starting transfers between devices  14.9 us (1%)
  between operations  14.3 us (1%)
    all_to_all x1, waiting for transfers between devices, on_device(): lax.all_to_all(payload.reshape(owner_count, send_cap, 2, block_size, bloc...  722 us
    scatter x1, local copies, waits for them, and re-layouts, on_device(): placed.at[received_ids.reshape(-1)]  92.4 us
    scatter x1, local copies, waits for them, and re-layouts, on_device(): payload = jnp.zeros((owner_count * send_cap, 2, block_size, block_size),...  45.3 us
    psum x1, waiting for transfers between devices, on_device(): lax.psum(jnp.concatenate([gate_part, up_part, down_part, sample_part], ax...  45.1 us
    convert_element_type x1, other arithmetic, on_device(): update.astype(jnp.bfloat16).reshape(state_shape)  33 us
  transfers between devices with their start and end apart: 3, of which 2 were waited for; matrix products, arithmetic and copies ran while one was open for 8% of the time, Pallas kernels for 0%

commit v1 on v0

--- a/solution.py
+++ b/solution.py
@@ -1,7 +1,386 @@
+import functools
+
 import jax
 import jax.numpy as jnp
 from jax import lax
+from jax.experimental import pallas as pl
+from jax.experimental.pallas import tpu as pltpu
 from jax.sharding import PartitionSpec as P
+
+MESH = pl.DeviceIdType.MESH
+VMEM_BYTES = 60 * 1024 * 1024
+ZERO_ROW = 15
+
+
+def nt_dot(a, b):
+    return lax.dot_general(a, b, (((1,), (1,)), ((), ())), preferred_element_type=jnp.float32)
+
+
+def signals_kernel(
+    n, chunks, index_ref, tokens_ref, grads_ref, samples_ref, gate_hbm, up_hbm, down_hbm, meta_ref,
+    sig_ref, rows_ref, meta_all,
+    acts, gate_v, up_v, down_v, parts, from_sib, pair, from_x,
+    tile_sem, act_send, act_recv, meta_send, meta_recv, sib1_send, sib1_recv, pair_send, pair_recv,
+    z_send, z_recv, x_send, x_recv, s_send, s_recv,
+):
+    z, x, s = lax.axis_index("dp"), lax.axis_index("mp"), lax.axis_index("sub")
+    columns, keep = gate_v.shape[0], gate_v.shape[1]
+    quarter = columns // 4
+    per = quarter // chunks
+    local_rows, block = tokens_ref.shape[0], gate_v.shape[-1]
+    tokens = n * local_rows
+    blocks = tokens_ref.shape[1] // block
+    order = [2 * (1 - x) + (1 - s), 2 * (1 - x) + s, 2 * x + (1 - s), 2 * x + s]
+
+    def load(t, m):
+        where = pl.ds(order[t] * quarter, quarter)
+        source, target = ((gate_hbm, gate_v), (up_hbm, up_v), (down_hbm, down_v))[m]
+        return pltpu.make_async_copy(source.at[where], target.at[where], tile_sem.at[t, m])
+
+    for t in range(4):
+        for m in range(3):
+            load(t, m).start()
+
+    barrier = pltpu.get_barrier_semaphore()
+    for d in range(1, n):
+        pl.semaphore_signal(
+            barrier, inc=1, device_id={"dp": lax.rem(z + d, n)}, device_id_type=MESH
+        )
+    pl.semaphore_signal(barrier, inc=1, device_id={"mp": 1 - x}, device_id_type=MESH)
+    pl.semaphore_signal(barrier, inc=1, device_id={"sub": 1 - s}, device_id_type=MESH)
+
+    own_rows = pl.ds(pl.multiple_of(z * local_rows, local_rows), local_rows)
+    for a, ref in enumerate((tokens_ref, grads_ref, samples_ref)):
+        for b in range(blocks):
+            acts[a * blocks + b, own_rows, :] = ref[:, b * block : (b + 1) * block]
+    meta_all[z] = meta_ref[...]
+    pl.semaphore_wait(barrier, n + 1)
+
+    def remote(source, target, send, recv, device):
+        return pltpu.make_async_remote_copy(
+            src_ref=source, dst_ref=target, send_sem=send, recv_sem=recv,
+            device_id=device, device_id_type=MESH,
+        )
+
+    def act_copy(d, origin):
+        where = pl.ds(pl.multiple_of(origin * local_rows, local_rows), local_rows)
+        view = acts.at[:, where, :]
+        return remote(
+            view, view, act_send.at[d - 1], act_recv.at[d - 1], {"dp": lax.rem(z + d, n)}
+        )
+
+    def meta_copy(d, origin):
+        view = meta_all.at[origin]
+        return remote(
+            view, view, meta_send.at[d - 1], meta_recv.at[d - 1], {"dp": lax.rem(z + d, n)}
+        )
+
+    for d in range(1, n):
+        act_copy(d, z).start()
+    for d in range(1, n):
+        meta_copy(d, z).start()
+    for d in range(1, n):
+        act_copy(d, lax.rem(z + n - d, n)).wait_recv()
+
+    def compute(c, at):
+        def row(m, k):
+            return lax.rem(index_ref[(m * columns + c) * keep + k], blocks)
+
+        for m, tile_ref in ((0, gate_v), (1, up_v)):
+            lhs = jnp.concatenate([acts[row(m, k)] for k in range(keep)], axis=1)
+            rhs = tile_ref[c].reshape(keep * block, block)
+            product = jnp.dot(lhs, rhs, preferred_element_type=jnp.float32)
+            parts[at, m] = product.astype(jnp.bfloat16)
+        total = None
+        for k in range(keep):
+            r = row(2, k)
+            lhs = jnp.concatenate([acts[blocks + r], acts[2 * blocks + r]], axis=0)
+            term = nt_dot(lhs, down_v[c, k])
+            total = term if total is None else total + term
+        parts[at, 2] = total[:tokens].astype(jnp.bfloat16)
+        parts[at, 3] = total[tokens:].astype(jnp.bfloat16)
+
+    def sib_part(i, j):
+        return remote(
+            parts.at[pl.ds(2 * i * quarter + j * per, per)],
+            from_sib.at[pl.ds(i * quarter + j * per, per)],
+            sib1_send.at[i, j], sib1_recv.at[i, j], {"sub": 1 - s},
+        )
+
+    def pair_copy(j):
+        where = pl.ds(j * per, per)
+        return remote(
+            pair.at[where], from_x.at[where], pair_send.at[j], pair_recv.at[j], {"mp": 1 - x}
+        )
+
+    for t in range(4):
+        for m in range(3):
+            load(t, m).wait()
+
+        def chunk_step(j, carry, t=t):
+            def one(u, inner):
+                cc = j * per + u
+                compute(order[t] * quarter + cc, t * quarter + cc)
+                return inner
+
+            lax.fori_loop(0, per, one, 0)
+            if t in (0, 2):
+                sib_part(t // 2, j).start()
+            if t == 1:
+                sib_part(0, j).wait_recv()
+
+                def add(u, inner):
+                    cc = j * per + u
+                    pair[cc] = (
+                        parts[quarter + cc].astype(jnp.float32)
+                        + from_sib[cc].astype(jnp.float32)
+                    ).astype(jnp.bfloat16)
+                    return inner
+
+                lax.fori_loop(0, per, add, 0)
+                pair_copy(j).start()
+            return carry
+
+        lax.fori_loop(0, chunks, chunk_step, 0)
+
+    for b in range(blocks):
+        rows_ref[b] = acts[b].astype(jnp.float32).T.astype(jnp.bfloat16)
+    for b in range(blocks, rows_ref.shape[0]):
+        rows_ref[b] = jnp.zeros(rows_ref.shape[1:], jnp.bfloat16)
+
+    def place(origin, xq, sq, j):
+        first = (origin * columns + (2 * xq + sq) * quarter + j * per) * 2
+        return sig_ref.at[pl.ds(first, 2 * per)]
+
+    def z_copy(way, d, j, origin):
+        side = (1 - way) // 2
+        view = place(origin, x, s, j)
+        return remote(
+            view, view, z_send.at[side, d - 1, j], z_recv.at[side, d - 1, j], {"dp": z + way}
+        )
+
+    def x_copy(xq, origin, j):
+        view = place(origin, xq, s, j)
+        return remote(view, view, x_send.at[origin, j], x_recv.at[origin, j], {"mp": 1 - x})
+
+    def s_copy(xq, sq, origin, j):
+        view = place(origin, xq, sq, j)
+        return remote(
+            view, view, s_send.at[xq, origin, j], s_recv.at[xq, origin, j], {"sub": 1 - s}
+        )
+
+    def inside(at):
+        return (at >= 0) & (at < n)
+
+    def produce(j):
+        sib_part(1, j).wait_recv()
+        pair_copy(j).wait_recv()
+
+        def one(u, inner):
+            cc = j * per + u
+            gate_sum, up_sum, hidden, sample = [
+                parts[3 * quarter + cc, a].astype(jnp.float32)
+                + from_sib[quarter + cc, a].astype(jnp.float32)
+                + from_x[cc, a].astype(jnp.float32)
+                for a in range(4)
+            ]
+            sig = jax.nn.sigmoid(gate_sum)
+            act = gate_sum * sig
+            slope = up_sum * sig * (1.0 + gate_sum * (1.0 - sig))
+            at = (z * columns + (2 * x + s) * quarter + cc) * 2
+            sig_ref[at, :, 0:block] = (hidden * slope).astype(jnp.bfloat16)
+            sig_ref[at, :, block : 2 * block] = (sample * slope).astype(jnp.bfloat16)
+            sig_ref[at + 1, :, 0:block] = (hidden * act).astype(jnp.bfloat16)
+            sig_ref[at + 1, :, block : 2 * block] = (sample * act).astype(jnp.bfloat16)
+            return inner
+
+        lax.fori_loop(0, per, one, 0)
+
+    def x_arrivals(d, j):
+        for way in (1, -1) if d else (1,):
+            origin = z - way * d
+
+            @pl.when(inside(origin))
+            def _():
+                x_copy(1 - x, origin, j).wait_recv()
+                s_copy(1 - x, s, origin, j).start()
+
+    for d in range(n):
+
+        def spread(j, carry, d=d):
+            if d == 0:
+                produce(j)
+                x_copy(x, z, j).start()
+                for way in (1, -1):
+
+                    @pl.when(inside(z + way))
+                    def _():
+                        z_copy(way, 1, j, z).start()
+
+                s_copy(x, s, z, j).start()
+                return carry
+            for way in (1, -1):
+                origin = z - way * d
+
+                @pl.when(inside(origin))
+                def _():
+                    z_copy(way, d, j, origin).wait_recv()
+                    if d < n - 1:
+
+                        @pl.when(inside(z + way))
+                        def _():
+                            z_copy(way, d + 1, j, origin).start()
+
+                    x_copy(x, origin, j).start()
+                    s_copy(x, s, origin, j).start()
+
+            x_arrivals(d - 1, j)
+            return carry
+
+        lax.fori_loop(0, chunks, spread, 0)
+
+    def finish(j, carry):
+        x_arrivals(n - 1, j)
+        return carry
+
+    lax.fori_loop(0, chunks, finish, 0)
+
+    for d in range(1, n):
+        meta_copy(d, lax.rem(z + n - d, n)).wait_recv()
+        act_copy(d, z).wait_send()
+        meta_copy(d, z).wait_send()
+
+    def drain(j, carry):
+        sib_part(0, j).wait_send()
+        sib_part(1, j).wait_send()
+        pair_copy(j).wait_send()
+        for d in range(1, n):
+            for way in (1, -1):
+                origin = z - way * (d - 1)
+
+                @pl.when(inside(origin) & inside(z + way))
+                def _():
+                    z_copy(way, d, j, origin).wait_send()
+
+        for origin in range(n):
+            x_copy(x, origin, j).wait_send()
+            for xq in range(2):
+                s_copy(xq, s, origin, j).wait_send()
+                s_copy(xq, 1 - s, origin, j).wait_recv()
+        return carry
+
+    lax.fori_loop(0, chunks, drain, 0)
+
+
+def update_kernel(per_step, table_ref, sig_ref, rows_ref, moment_ref, curvature_ref, m_out, c_out, u_out):
+    step = pl.program_id(0)
+    block = moment_ref.shape[-1]
+
+    def one(u, carry):
+        code = table_ref[step * per_step + u]
+        lhs = rows_ref[code & 15]
+        rhs = sig_ref[code >> 4]
+        product = jnp.dot(lhs, rhs, preferred_element_type=jnp.float32)
+        product = product.astype(jnp.bfloat16).astype(jnp.float32)
+        grad, hat = product[:, :block], product[:, block:]
+        moment = 0.9 * moment_ref[u].astype(jnp.float32) + (1.0 - 0.9) * grad
+        curvature = 0.95 * curvature_ref[u].astype(jnp.float32) + (1.0 - 0.95) * hat * hat
+        m_out[u] = moment.astype(jnp.bfloat16)
+        c_out[u] = curvature.astype(jnp.bfloat16)
+        u_out[u] = jnp.clip(moment / (0.5 * curvature), -1.0, 1.0).astype(jnp.bfloat16)
+        return carry
+
+    lax.fori_loop(0, per_step, one, 0, unroll=4)
+
+
+def factor_exchange(
+    tokens_in, grad_out, sample_grad, gate_tiles, up_tiles, down_tiles,
+    block_index, owner_map, slot_map, moment_state, curvature_state,
+):
+    n = lax.axis_size("dp")
+    columns, keep, block, _ = gate_tiles.shape
+    local_rows, width = tokens_in.shape
+    tokens, blocks = n * local_rows, width // block
+    own_cap = moment_state.shape[2]
+    quarter = columns // 4
+    chunks = 4
+    z = lax.axis_index("dp")
+    band = lax.axis_index(("mp", "sub"))
+    key = owner_map * own_cap + slot_map
+    column = z * columns + jnp.arange(columns, dtype=jnp.int32)
+    entry = column[None, :, None] * 2 + jnp.arange(2, dtype=jnp.int32)[:, None, None]
+    code = entry * 16 + block_index[:2] - band * blocks
+    lanes = 2 * columns * keep // 8
+    meta = jnp.stack([key.reshape(8, lanes), code.reshape(8, lanes)])
+    vmem, hbm, smem = (
+        pl.BlockSpec(memory_space=pltpu.VMEM),
+        pl.BlockSpec(memory_space=pl.ANY),
+        pl.BlockSpec(memory_space=pltpu.SMEM),
+    )
+    bf16, dma = jnp.bfloat16, pltpu.SemaphoreType.DMA
+    sig, rows, meta_all = pl.pallas_call(
+        functools.partial(signals_kernel, n, chunks),
+        out_shape=(
+            jax.ShapeDtypeStruct((n * columns * 2, tokens, 2 * block), bf16),
+            jax.ShapeDtypeStruct((16, block, tokens), bf16),
+            jax.ShapeDtypeStruct((n, 2, 8, lanes), jnp.int32),
+        ),
+        in_specs=[smem, vmem, vmem, vmem, hbm, hbm, hbm, vmem],
+        out_specs=(vmem, vmem, vmem),
+        scratch_shapes=[
+            pltpu.VMEM((3 * blocks, tokens, block), bf16),
+            pltpu.VMEM(gate_tiles.shape, bf16),
+            pltpu.VMEM(gate_tiles.shape, bf16),
+            pltpu.VMEM(gate_tiles.shape, bf16),
+            pltpu.VMEM((columns, 4, tokens, block), bf16),
+            pltpu.VMEM((2 * quarter, 4, tokens, block), bf16),
+            pltpu.VMEM((quarter, 4, tokens, block), bf16),
+            pltpu.VMEM((quarter, 4, tokens, block), bf16),
+            dma((4, 3)),
+            dma((n - 1,)), dma((n - 1,)), dma((n - 1,)), dma((n - 1,)),
+            dma((2, chunks)), dma((2, chunks)), dma((chunks,)), dma((chunks,)),
+            dma((2, n - 1, chunks)), dma((2, n - 1, chunks)),
+            dma((n, chunks)), dma((n, chunks)),
+            dma((2, n, chunks)), dma((2, n, chunks)),
+        ],
+        compiler_params=pltpu.CompilerParams(
+            collective_id=0, has_side_effects=True, vmem_limit_bytes=VMEM_BYTES
+        ),
+        name="signals",
+    )(
+        block_index.reshape(-1), tokens_in, grad_out, sample_grad,
+        gate_tiles, up_tiles, down_tiles, meta,
+    )
+    keys = meta_all[:, 0].reshape(-1) - z * own_cap
+    codes = meta_all[:, 1].reshape(-1)
+    match = keys[None, :] == jnp.arange(own_cap, dtype=jnp.int32)[:, None]
+    table = jnp.sum(jnp.where(match, codes[None, :] - ZERO_ROW, 0), axis=1) + ZERO_ROW
+    per_step = 16
+    state = pl.BlockSpec((per_step, block, block), lambda i, t: (i, 0, 0))
+    once = pl.Buffered(1)
+    outs = pl.pallas_call(
+        functools.partial(update_kernel, per_step),
+        out_shape=[jax.ShapeDtypeStruct((own_cap, block, block), bf16)] * 3,
+        grid_spec=pltpu.PrefetchScalarGridSpec(
+            num_scalar_prefetch=1,
+            grid=(own_cap // per_step,),
+            in_specs=[
+                pl.BlockSpec(sig.shape, lambda i, t: (0, 0, 0), pipeline_mode=once),
+                pl.BlockSpec(rows.shape, lambda i, t: (0, 0, 0), pipeline_mode=once),
+                state,
+                state,
+            ],
+            out_specs=[state] * 3,
+        ),
+        compiler_params=pltpu.CompilerParams(vmem_limit_bytes=VMEM_BYTES),
+        name="update",
+    )(
+        table, sig, rows,
+        moment_state.reshape(own_cap, block, block),
+        curvature_state.reshape(own_cap, block, block),
+    )
+    return tuple(out.reshape(moment_state.shape) for out in outs)
+
 
 momentum_decay = 0.9
 curvature_decay = 0.95
@@ -10,7 +389,8 @@
 
 def pick_blocks(matrix, row_list, block_size):
     shaped = matrix.reshape(matrix.shape[0], matrix.shape[1] // block_size, block_size)
-    return jnp.take(shaped, row_list, axis=1)
+    chosen = row_list[..., None] == jnp.arange(shaped.shape[1], dtype=row_list.dtype)
+    return jnp.einsum("tbd,ckb->tckd", shaped, chosen.astype(matrix.dtype))
 
 
 def backward_signals(summed):
@@ -33,7 +413,7 @@
     ).astype(jnp.bfloat16)
 
 
-def on_device(
+def tile_exchange(
     tokens_in,
     grad_out,
     sample_grad,
@@ -181,6 +561,15 @@
         P(("groups", "dp"), ("mp", "sub"), None, None, None),
         P(("groups", "dp"), ("mp", "sub"), None, None, None),
     )
+    factors = mesh.shape["mp"] == 2 and mesh.shape["sub"] == 2
+
+    def on_device(*args):
+        columns, _, block_size, _ = args[3].shape
+        tokens = args[0].shape[0] * mesh.shape["dp"]
+        own_cap = args[9].shape[2]
+        fits = tokens <= block_size and columns % 16 == 0 and own_cap % 16 == 0
+        return (factor_exchange if factors and fits else tile_exchange)(*args)
+
     return jax.shard_map(
         on_device, mesh=mesh, in_specs=in_specs, out_specs=out_specs, check_vma=False
     )

time: 1080 us -> 129 us (0.12)
  waiting for transfers between devices: 768 us -> 0 us
  local copies, waits for them, and re-layouts: 179 us -> 1.96 us
  Pallas kernels: 0 us -> 121 us
  blocking collectives: 42.2 us -> 0 us
  other arithmetic: 43.6 us -> 3.58 us
  matrix products: 18.5 us -> 0 us
  starting transfers between devices: 14.9 us -> 0 us
  between operations: 14.3 us -> 0.67 us
    all_to_all x2 -> x0, waiting for transfers between devices: 722 us -> none  [the longest x1 722 us: on_device(): lax.all_to_all(payload.reshape(owner_count, send_cap, 2, block_size, bloc...]
    scatter x3 -> x0, local copies, waits for them, and re-layouts: 140 us -> none  [the longest x1 92.4 us: on_device(): placed.at[received_ids.reshape(-1)]]
    pallas_call x0 -> x2, Pallas kernels: none -> 121 us  [the longest x1 80.5 us: factor_exchange(): pl.pallas_call(functools.partial(signals_kernel, n, chunks), out_shape=(j...]
    psum x1 -> x0, waiting for transfers between devices: 45.1 us -> none  [on_device(): lax.psum(jnp.concatenate([gate_part, up_part, down_part, sample_part], ax...]
    all_gather x3 -> x0, blocking collectives: 42.2 us -> none  [the longest x1 15.3 us: on_device(): lax.all_gather(tokens_in, 'dp', axis=0, tiled=True)]
    convert_element_type x3 -> x0, other arithmetic: 36.5 us -> none  [the longest x1 33 us: on_device(): update.astype(jnp.bfloat16).reshape(state_shape)]
    broadcast_in_dim x5 -> x0, local copies, waits for them, and re-layouts: 20.7 us -> none  [the longest x1 11.3 us: on_device(): jnp.zeros((owner_count * send_cap, 2, block_size, block_size), jnp.bfloat16)]
    dot_general x8 -> x0, matrix products: 18.5 us -> none  [the longest x1 4.58 us: on_device(): jnp.einsum('tckd,cked->tce', pick_blocks(all_grads, local_rows[2], block_...]
  transfers between devices with their start and end apart: 3 -> 0, of which waited for: 2 -> 0; matrix products, arithmetic and copies ran while one was open for 8% -> 0% of each run, Pallas kernels for 0% -> 0%
where the time goes in v1:
time: 129 us; the launch traced here: 127 us
  Pallas kernels  121 us (94%)
  other arithmetic  3.58 us (3%)
  local copies, waits for them, and re-layouts  1.96 us (2%)
    pallas_call x1, Pallas kernels, factor_exchange(): pl.pallas_call(functools.partial(signals_kernel, n, chunks), out_shape=(j...  80.5 us
    pallas_call x1, Pallas kernels, factor_exchange(): pl.pallas_call(functools.partial(update_kernel, per_step), out_shape=[jax...  40.4 us

profile of v1, /device:TPU:0, one launch (start us, length us, event | category | flops | bytes accessed | tf_op | source)
XLA Modules:
  0.0 127.1 jit_solution(16959483688731510204)
XLA Ops:
  0.7 0.7 add_subtract_fusion
  1.4 0.7 multiply_add_fusion
  2.1 0.1 copy.20
  2.2 0.1 stack_reshape.6
  2.2 0.1 copy.21
  2.3 0.1 stack_reshape.7
  2.4 0.6 pad_add_fusion.meta_ref
  3.0 0.8 copy.19
  3.8 0.7 reshape.71.index_ref
  4.5 80.5 %signals.1 = (bf16[256,64,256]{2,1,0:T(8,128)(2,1)}, bf16[16,128,64]{2,1,0:T(8,128)(2,1)}, s32[4,2,8,32]{3,2,1,0:T(8,128)}) custom-call(s32[384]{0:T(512)} %reshape.71.index_ref, bf16[16,1024]{1,0:T(8,128)(2,1)} %tokens_ref.1, bf16[16,1024]{1,0:T(8,128)(2,1)} %grads_ref.1, bf16[16,1024]{1,0:T(8,128)(2,1)} %samples_ref.1, bf16[32,4,128,128]{3,2,1,0:T(8,128)(2,1)} %gate_hbm.1, ...), custom_call_target="tpu_custom_call" | custom-call | tf_op jit(solution)/shard_map/signals/pallas_call | solution.py:321
  85.0 0.7 slice_subtract_fusion
  85.8 0.1 sub.29
  85.8 0.1 sub.31
  85.9 0.2 select_reduce_fusion
  86.1 0.6 broadcast_add_fusion.table_ref
  86.7 40.4 %update.1 = (bf16[384,128,128]{2,1,0:T(8,128)(2,1)}, bf16[384,128,128]{2,1,0:T(8,128)(2,1)}, bf16[384,128,128]{2,1,0:T(8,128)(2,1)}) custom-call(s32[384]{0:T(512)} %broadcast_add_fusion.table_ref, bf16[256,64,256]{2,1,0:T(8,128)(2,1)} %get-tuple-element.10.sig_ref, bf16[16,128,64]{2,1,0:T(8,128)(2,1)} %get-tuple-element.11.rows_ref, ...), custom_call_target="tpu_custom_call" | custom-call | tf_op jit(solution)/shard_map/update/pallas_call | solution.py:361
  (2 shorter events, 0.0 us)

commit v2 on v1

--- a/solution.py
+++ b/solution.py
@@ -17,9 +17,10 @@
 
 
 def signals_kernel(
-    n, chunks, index_ref, tokens_ref, grads_ref, samples_ref, gate_hbm, up_hbm, down_hbm, meta_ref,
-    sig_ref, rows_ref, meta_all,
-    acts, gate_v, up_v, down_v, parts, from_sib, pair, from_x,
+    n, chunks, own_cap, index_ref, tokens_ref, grads_ref, samples_ref, gate_hbm, up_hbm, down_hbm,
+    owner_ref, slot_ref, block_ref,
+    sig_ref, rows_ref, table_ref,
+    acts, meta_all, gate_v, up_v, down_v, parts, from_sib, pair, from_x,
     tile_sem, act_send, act_recv, meta_send, meta_recv, sib1_send, sib1_recv, pair_send, pair_recv,
     z_send, z_recv, x_send, x_recv, s_send, s_recv,
 ):
@@ -41,6 +42,7 @@
         for m in range(3):
             load(t, m).start()
 
+    meta_all[...] = jnp.full(meta_all.shape, -1, jnp.int32)
     barrier = pltpu.get_barrier_semaphore()
     for d in range(1, n):
         pl.semaphore_signal(
@@ -53,7 +55,15 @@
     for a, ref in enumerate((tokens_ref, grads_ref, samples_ref)):
         for b in range(blocks):
             acts[a * blocks + b, own_rows, :] = ref[:, b * block : (b + 1) * block]
-    meta_all[z] = meta_ref[...]
+    lists = 2 * keep
+    for m in range(2):
+        column = lax.broadcasted_iota(jnp.int32, (keep, columns), 1) + z * columns
+        code = (column * 2 + m) * 16 + block_ref[m] - (2 * x + s) * blocks
+        key = owner_ref[m] * own_cap + slot_ref[m]
+        for k in range(keep):
+            at = pl.ds(z * lists + m * keep + k, 1)
+            meta_all[0, at, 0:columns] = key[k : k + 1]
+            meta_all[1, at, 0:columns] = code[k : k + 1]
     pl.semaphore_wait(barrier, n + 1)
 
     def remote(source, target, send, recv, device):
@@ -70,7 +80,7 @@
         )
 
     def meta_copy(d, origin):
-        view = meta_all.at[origin]
+        view = meta_all.at[:, pl.ds(pl.multiple_of(origin * lists, lists), lists), :]
         return remote(
             view, view, meta_send.at[d - 1], meta_recv.at[d - 1], {"dp": lax.rem(z + d, n)}
         )
@@ -84,7 +94,7 @@
 
     def compute(c, at):
         def row(m, k):
-            return lax.rem(index_ref[(m * columns + c) * keep + k], blocks)
+            return lax.rem(index_ref[m, k, c], blocks)
 
         for m, tile_ref in ((0, gate_v), (1, up_v)):
             lhs = jnp.concatenate([acts[row(m, k)] for k in range(keep)], axis=1)
@@ -143,21 +153,32 @@
 
         lax.fori_loop(0, chunks, chunk_step, 0)
 
+    for d in range(1, n):
+        meta_copy(d, lax.rem(z + n - d, n)).wait_recv()
+    keys = meta_all[0].astype(jnp.float32).T[:columns] - (z * own_cap).astype(jnp.float32)
+    codes = meta_all[1].astype(jnp.float32).T[:columns] - ZERO_ROW
+    slots = lax.broadcasted_iota(jnp.int32, (columns, own_cap), 1).astype(jnp.float32)
+    found = jnp.zeros((columns, own_cap), jnp.float32)
+    for r in range(n * lists):
+        found += jnp.where(keys[:, r : r + 1] == slots, codes[:, r : r + 1], 0.0)
+    table_ref[...] = (jnp.sum(found, axis=0, keepdims=True) + ZERO_ROW).astype(jnp.int32)
+
     for b in range(blocks):
         rows_ref[b] = acts[b].astype(jnp.float32).T.astype(jnp.bfloat16)
     for b in range(blocks, rows_ref.shape[0]):
         rows_ref[b] = jnp.zeros(rows_ref.shape[1:], jnp.bfloat16)
 
+    shared = chunks // 4
+
     def place(origin, xq, sq, j):
         first = (origin * columns + (2 * xq + sq) * quarter + j * per) * 2
         return sig_ref.at[pl.ds(first, 2 * per)]
 
-    def z_copy(way, d, j, origin):
+    def z_copy(way, d, j, origin, other=False):
         side = (1 - way) // 2
-        view = place(origin, x, s, j)
-        return remote(
-            view, view, z_send.at[side, d - 1, j], z_recv.at[side, d - 1, j], {"dp": z + way}
-        )
+        view = place(origin, 1 - x if other else x, s, j)
+        at = (side, d - 1, chunks + j if other else j)
+        return remote(view, view, z_send.at[at], z_recv.at[at], {"dp": z + way})
 
     def x_copy(xq, origin, j):
         view = place(origin, xq, s, j)
@@ -231,22 +252,47 @@
                         def _():
                             z_copy(way, d + 1, j, origin).start()
 
-                    x_copy(x, origin, j).start()
+                    @pl.when(j >= shared)
+                    def _():
+                        x_copy(x, origin, j).start()
+
                     s_copy(x, s, origin, j).start()
 
-            x_arrivals(d - 1, j)
+            @pl.when(j >= shared)
+            def _():
+                x_arrivals(d - 1, j)
+
             return carry
 
         lax.fori_loop(0, chunks, spread, 0)
+        for f in range(shared):
+            if d == 0:
+                x_copy(1 - x, z, f).wait_recv()
+            for way in (1, -1):
+                origin = z - way * d
+
+                @pl.when(inside(origin))
+                def _():
+                    if d > 0:
+                        z_copy(way, d, f, origin, True).wait_recv()
+                    if d < n - 1:
+
+                        @pl.when(inside(z + way))
+                        def _():
+                            z_copy(way, d + 1, f, origin, True).start()
+
+                    if d > 0:
+                        s_copy(1 - x, s, origin, f).start()
+            if d == 0:
+                s_copy(1 - x, s, z, f).start()
 
     def finish(j, carry):
         x_arrivals(n - 1, j)
         return carry
 
-    lax.fori_loop(0, chunks, finish, 0)
+    lax.fori_loop(shared, chunks, finish, 0)
 
     for d in range(1, n):
-        meta_copy(d, lax.rem(z + n - d, n)).wait_recv()
         act_copy(d, z).wait_send()
         meta_copy(d, z).wait_send()
 
@@ -262,8 +308,16 @@
                 def _():
                     z_copy(way, d, j, origin).wait_send()
 
+                    @pl.when(j < shared)
+                    def _():
+                        z_copy(way, d, j, origin, True).wait_send()
+
         for origin in range(n):
-            x_copy(x, origin, j).wait_send()
+
+            @pl.when((j >= shared) | (z == origin))
+            def _():
+                x_copy(x, origin, j).wait_send()
+
             for xq in range(2):
                 s_copy(xq, s, origin, j).wait_send()
                 s_copy(xq, 1 - s, origin, j).wait_recv()
@@ -290,7 +344,7 @@
         u_out[u] = jnp.clip(moment / (0.5 * curvature), -1.0, 1.0).astype(jnp.bfloat16)
         return carry
 
-    lax.fori_loop(0, per_step, one, 0, unroll=4)
+    lax.fori_loop(0, per_step, one, 0, unroll=16 if per_step % 16 == 0 else 1)
 
 
 def factor_exchange(
@@ -304,31 +358,25 @@
     own_cap = moment_state.shape[2]
     quarter = columns // 4
     chunks = 4
-    z = lax.axis_index("dp")
-    band = lax.axis_index(("mp", "sub"))
-    key = owner_map * own_cap + slot_map
-    column = z * columns + jnp.arange(columns, dtype=jnp.int32)
-    entry = column[None, :, None] * 2 + jnp.arange(2, dtype=jnp.int32)[:, None, None]
-    code = entry * 16 + block_index[:2] - band * blocks
-    lanes = 2 * columns * keep // 8
-    meta = jnp.stack([key.reshape(8, lanes), code.reshape(8, lanes)])
+    owner_t, slot_t, index_t = [a.transpose(0, 2, 1) for a in (owner_map, slot_map, block_index)]
     vmem, hbm, smem = (
         pl.BlockSpec(memory_space=pltpu.VMEM),
         pl.BlockSpec(memory_space=pl.ANY),
         pl.BlockSpec(memory_space=pltpu.SMEM),
     )
     bf16, dma = jnp.bfloat16, pltpu.SemaphoreType.DMA
-    sig, rows, meta_all = pl.pallas_call(
-        functools.partial(signals_kernel, n, chunks),
+    sig, rows, table = pl.pallas_call(
+        functools.partial(signals_kernel, n, chunks, own_cap),
         out_shape=(
             jax.ShapeDtypeStruct((n * columns * 2, tokens, 2 * block), bf16),
             jax.ShapeDtypeStruct((16, block, tokens), bf16),
-            jax.ShapeDtypeStruct((n, 2, 8, lanes), jnp.int32),
+            jax.ShapeDtypeStruct((1, own_cap), jnp.int32),
         ),
-        in_specs=[smem, vmem, vmem, vmem, hbm, hbm, hbm, vmem],
+        in_specs=[smem, vmem, vmem, vmem, hbm, hbm, hbm, vmem, vmem, vmem],
         out_specs=(vmem, vmem, vmem),
         scratch_shapes=[
             pltpu.VMEM((3 * blocks, tokens, block), bf16),
+            pltpu.VMEM((2, 128, 128), jnp.int32),
             pltpu.VMEM(gate_tiles.shape, bf16),
             pltpu.VMEM(gate_tiles.shape, bf16),
             pltpu.VMEM(gate_tiles.shape, bf16),
@@ -339,7 +387,7 @@
             dma((4, 3)),
             dma((n - 1,)), dma((n - 1,)), dma((n - 1,)), dma((n - 1,)),
             dma((2, chunks)), dma((2, chunks)), dma((chunks,)), dma((chunks,)),
-            dma((2, n - 1, chunks)), dma((2, n - 1, chunks)),
+            dma((2, n - 1, chunks + chunks // 4)), dma((2, n - 1, chunks + chunks // 4)),
             dma((n, chunks)), dma((n, chunks)),
             dma((2, n, chunks)), dma((2, n, chunks)),
         ],
@@ -348,14 +396,10 @@
         ),
         name="signals",
     )(
-        block_index.reshape(-1), tokens_in, grad_out, sample_grad,
-        gate_tiles, up_tiles, down_tiles, meta,
-    )
-    keys = meta_all[:, 0].reshape(-1) - z * own_cap
-    codes = meta_all[:, 1].reshape(-1)
-    match = keys[None, :] == jnp.arange(own_cap, dtype=jnp.int32)[:, None]
-    table = jnp.sum(jnp.where(match, codes[None, :] - ZERO_ROW, 0), axis=1) + ZERO_ROW
-    per_step = 16
+        index_t, tokens_in, grad_out, sample_grad,
+        gate_tiles, up_tiles, down_tiles, owner_t, slot_t, index_t,
+    )
+    per_step = max(p for p in range(1, 65) if own_cap % p == 0)
     state = pl.BlockSpec((per_step, block, block), lambda i, t: (i, 0, 0))
     once = pl.Buffered(1)
     outs = pl.pallas_call(
@@ -375,7 +419,7 @@
         compiler_params=pltpu.CompilerParams(vmem_limit_bytes=VMEM_BYTES),
         name="update",
     )(
-        table, sig, rows,
+        table.reshape(own_cap), sig, rows,
         moment_state.reshape(own_cap, block, block),
         curvature_state.reshape(own_cap, block, block),
     )
@@ -568,6 +612,7 @@
         tokens = args[0].shape[0] * mesh.shape["dp"]
         own_cap = args[9].shape[2]
         fits = tokens <= block_size and columns % 16 == 0 and own_cap % 16 == 0
+        fits = fits and columns <= 128 and 2 * args[3].shape[1] * mesh.shape["dp"] <= 128
         return (factor_exchange if factors and fits else tile_exchange)(*args)
 
     return jax.shard_map(

time: 129 us -> 110 us (0.85); the launches traced: 127 us -> 110 us
  Pallas kernels: 121 us -> 108 us
  other arithmetic: 3.58 us -> 1.25 us
  local copies, waits for them, and re-layouts: 1.96 us -> 0 us
    pallas_call x1, Pallas kernels: 40.4 us -> 30.5 us  [factor_exchange(): pl.pallas_call(functools.partial(update_kernel, per_step), out_shape=[jax...]
    pallas_call x1, Pallas kernels: 80.5 us -> 77.7 us  [factor_exchange(): pl.pallas_call(functools.partial(signals_kernel, n, chunks, own_cap), out...]
    sub x2 -> x0, other arithmetic: 1.44 us -> none  [the longest x1 0.74 us: factor_exchange(): keys = meta_all[:, 0].reshape(-1) - z * own_cap]
where the time goes in v2:
time: 110 us
  Pallas kernels  108 us (98%)
  other arithmetic  1.25 us (1%)
    pallas_call x1, Pallas kernels, factor_exchange(): pl.pallas_call(functools.partial(signals_kernel, n, chunks, own_cap), out...  77.7 us
    pallas_call x1, Pallas kernels, factor_exchange(): pl.pallas_call(functools.partial(update_kernel, per_step), out_shape=[jax...  30.5 us

profile of v2, /device:TPU:0, one launch (start us, length us, event | category | flops | bytes accessed | tf_op | source)
XLA Modules:
  0.0 110.0 jit_solution(1136416131573708325)
XLA Ops:
  0.6 77.7 %signals.1 = (bf16[256,64,256]{2,1,0:T(8,128)(2,1)}, bf16[16,128,64]{2,1,0:T(8,128)(2,1)}, s32[1,384]{1,0:T(1,128)}) custom-call(s32[3,4,32]{2,1,0:T(4,128)} %bitcast.10, bf16[16,1024]{1,0:T(8,128)(2,1)} %tokens_ref.1, bf16[16,1024]{1,0:T(8,128)(2,1)} %grads_ref.1, bf16[16,1024]{1,0:T(8,128)(2,1)} %samples_ref.1, bf16[32,4,128,128]{3,2,1,0:T(8,128)(2,1)} %gate_hbm.1, ...), custom_call_target="tpu_custom_call" | custom-call | tf_op jit(solution)/shard_map/signals/pallas_call | solution.py:368
  78.3 1.2 %reduce.table_ref = s32[384]{0:T(512)} reduce(s32[1,384]{1,0:T(1,128)} %get-tuple-element.9, s32[]{:T(128)} %constant.3), dimensions={0}, to_apply=%get-tuple-element.9.reduce_sub_computation | reduce | bytes 3076 | tf_op jit(solution)/shard_map/signals/pallas_call | solution.py:368
  79.6 30.5 %update.1 = (bf16[384,128,128]{2,1,0:T(8,128)(2,1)}, bf16[384,128,128]{2,1,0:T(8,128)(2,1)}, bf16[384,128,128]{2,1,0:T(8,128)(2,1)}) custom-call(s32[384]{0:T(512)} %reduce.table_ref, bf16[256,64,256]{2,1,0:T(8,128)(2,1)} %get-tuple-element.10.sig_ref, bf16[16,128,64]{2,1,0:T(8,128)(2,1)} %get-tuple-element.11.rows_ref, bf16[384,128,128]{2,1,0:T(8,128)(2,1)} %bitcast.8, ...), custom_call_target="tpu_custom_call" | custom-call | tf_op jit(solution)/shard_map/update/pallas_call | solution.py:405

commit v3 on v2

--- a/solution.py
+++ b/solution.py
@@ -331,7 +331,7 @@
     block = moment_ref.shape[-1]
 
     def one(u, carry):
-        code = table_ref[step * per_step + u]
+        code = table_ref[0, step * per_step + u]
         lhs = rows_ref[code & 15]
         rhs = sig_ref[code >> 4]
         product = jnp.dot(lhs, rhs, preferred_element_type=jnp.float32)
@@ -357,7 +357,7 @@
     tokens, blocks = n * local_rows, width // block
     own_cap = moment_state.shape[2]
     quarter = columns // 4
-    chunks = 4
+    chunks = 8 if quarter % 8 == 0 else 4
     owner_t, slot_t, index_t = [a.transpose(0, 2, 1) for a in (owner_map, slot_map, block_index)]
     vmem, hbm, smem = (
         pl.BlockSpec(memory_space=pltpu.VMEM),
@@ -419,7 +419,7 @@
         compiler_params=pltpu.CompilerParams(vmem_limit_bytes=VMEM_BYTES),
         name="update",
     )(
-        table.reshape(own_cap), sig, rows,
+        table, sig, rows,
         moment_state.reshape(own_cap, block, block),
         curvature_state.reshape(own_cap, block, block),
     )

time: 110 us -> 110 us (level)
  other arithmetic: 1.25 us -> 0 us
    pallas_call x1 -> x0, other arithmetic: 1.25 us -> none  [factor_exchange(): pl.pallas_call(functools.partial(signals_kernel, n, chunks, own_cap), out...]
where the time goes in v3:
time: 110 us; the launch traced here: 109 us
  Pallas kernels  109 us (99%)
    pallas_call x1, Pallas kernels, factor_exchange(): pl.pallas_call(functools.partial(signals_kernel, n, chunks, own_cap), out...  78.4 us
    pallas_call x1, Pallas kernels, factor_exchange(): pl.pallas_call(functools.partial(update_kernel, per_step), out_shape=[jax...  30.5 us

profile of v3, /device:TPU:0, one launch (start us, length us, event | category | flops | bytes accessed | tf_op | source)
XLA Modules:
  0.0 109.5 jit_solution(2798626056632030479)
XLA Ops:
  0.6 78.4 %signals.1 = (bf16[256,64,256]{2,1,0:T(8,128)(2,1)}, bf16[16,128,64]{2,1,0:T(8,128)(2,1)}, s32[1,384]{1,0:T(1,128)}) custom-call(s32[3,4,32]{2,1,0:T(4,128)} %bitcast.10, bf16[16,1024]{1,0:T(8,128)(2,1)} %tokens_ref.1, bf16[16,1024]{1,0:T(8,128)(2,1)} %grads_ref.1, bf16[16,1024]{1,0:T(8,128)(2,1)} %samples_ref.1, bf16[32,4,128,128]{3,2,1,0:T(8,128)(2,1)} %gate_hbm.1, ...), custom_call_target="tpu_custom_call" | custom-call | tf_op jit(solution)/shard_map/signals/pallas_call | solution.py:368
  79.0 30.5 %update.1 = (bf16[384,128,128]{2,1,0:T(8,128)(2,1)}, bf16[384,128,128]{2,1,0:T(8,128)(2,1)}, bf16[384,128,128]{2,1,0:T(8,128)(2,1)}) custom-call(s32[1,384]{1,0:T(1,128)} %get-tuple-element.9.table_ref, bf16[256,64,256]{2,1,0:T(8,128)(2,1)} %get-tuple-element.10.sig_ref, bf16[16,128,64]{2,1,0:T(8,128)(2,1)} %get-tuple-element.11.rows_ref, ...), custom_call_target="tpu_custom_call" | custom-call | tf_op jit(solution)/shard_map/update/pallas_call | solution.py:405
